TPU v7x, 128 devices: a whole 4x4x4 slice. The times are simulated.
128 devices in a mesh: prow: 16 (over z, y), pcol: 8 (over x, core).
Axes of the slice: x: 4, y: 4, z: 4, core: 2. Of those that a mesh axis runs over, the one named last changes fastest.
Arguments:
- data: float32 [32768, 16384], P('prow', 'pcol'), may hold values from 0.05 to 5
- w_trans: float32 [32, 32768], P(None, ('prow', 'pcol')), as said below
- h_prior: float32 [32, 16384], P(None, 'pcol'), may hold values from 0.1 to 3
Outputs:
- h_next: float32 [32, 16384], P(None, 'pcol')
Inputs may be any that keep to these rules, and one draw needn't show every extreme that they name: `w_trans`: every entry is positive.
All inputs are finite; a program needn't handle non-finite values.
Results may differ from a plain program's by a relative error of at most 0.0003.
Values sent between devices are 32-bit elements; how exact they have to be, the bound alone decides.
A program may use at most 64 MiB of HBM per device.

v0:
```python
import jax
import jax.numpy as jnp
from jax import lax
from jax.sharding import PartitionSpec as P


def sweep(h_start, cross, gram):
    rank = h_start.shape[0]
    block = 8
    h_now = h_start
    for first in range(0, rank, block):
        mixed = jnp.dot(gram[first : first + block], h_now, precision=lax.Precision.HIGHEST)
        olds = h_now[first : first + block]
        fresh_rows = []
        for inner in range(block):
            k = first + inner
            total = mixed[inner]
            for prior in range(inner):
                total = total + gram[k, first + prior] * (fresh_rows[prior] - olds[prior])
            fresh = jnp.maximum(olds[inner] + (cross[k] - total) / gram[k, k], 0.0)
            fresh_rows.append(fresh)
        h_now = lax.dynamic_update_slice_in_dim(h_now, jnp.stack(fresh_rows, 0), first, 0)
    return h_now


def shards(data, w_trans, h_prior):
    cross_part = jnp.dot(
        lax.all_gather(w_trans, "pcol", axis=1, tiled=True), data, precision=lax.Precision.HIGHEST
    )
    own_gram = jnp.dot(w_trans, w_trans.T, precision=lax.Precision.HIGHEST)
    gram = lax.psum(own_gram, ("prow", "pcol"))
    cross = lax.psum(cross_part, "prow")
    return sweep(h_prior, cross, gram)


def solution(mesh):
    placed = (P("prow", "pcol"), P(None, ("prow", "pcol")), P(None, "pcol"))
    return jax.shard_map(
        shards, mesh=mesh, in_specs=placed, out_specs=P(None, "pcol"), check_vma=False
    )
```

profile of v0, /device:TPU:0, one launch (start us, length us, event | category | flops | bytes accessed | tf_op | source)
XLA Modules:
  0.0 228.7 jit_solution(6783842420621837805)
XLA Ops:
  6.5 1.0 copy.10
  7.5 13.5 %all_gather.3 = f32[32,2048]{1,0:T(8,128)S(1)} all-gather(f32[32,256]{1,0:T(8,128)} %param.4), channel_id=1, replica_groups=mesh['prow'=16,'pcol'=8] {'pcol'}, dimensions={1}, use_global_device_ids=true | all-gather | bytes 294912 | tf_op jit(solution)/shard_map/all_gather | solution.py:28
  21.0 13.8 %fusion.128 = f32[32,2048]{1,0:T(8,128)} fusion(f32[32,2048]{1,0:T(8,128)S(1)} %all_gather.3, f32[2048,2048]{1,0:T(8,128)} %param.3), kind=kOutput, calls=%fused_computation.212 | convolution fusion | flops 1610612736 | bytes 17301504 | tf_op jit(solution)/shard_map/dot_general | solution.py:27
  35.0 69.1 %psum.15 = f32[32,32]{1,0:T(8,128)S(1)} all-reduce(f32[32,32]{1,0:T(8,128)S(1)} %fusion.129), channel_id=1, replica_groups=mesh['prow'=16,'pcol'=8] {'prow','pcol'}, use_global_device_ids=true, to_apply=%region_1.0 | all-reduce | flops 1024 | bytes 8192 | tf_op jit(solution)/shard_map/psum | solution.py:31
  104.1 0.7 fusion.126
  104.8 0.7 fusion.125
  105.5 0.7 fusion.124
  106.2 0.7 fusion.123
  107.0 0.7 fusion.122
  107.7 0.7 fusion.120
  108.4 0.7 fusion.121
  109.1 0.7 fusion.127
  109.8 0.7 slice.1335
  110.5 0.2 fusion.90
  110.7 10.4 %all-reduce.2.cloned.1.call-done = f32[32,2048]{1,0:T(8,128)} async-done(((f32[32,2048]{1,0:T(8,128)}), f32[32,2048]{1,0:T(8,128)}) %all-reduce.2.cloned.1.call-update) | async-done | bytes 262160 | tf_op jit(solution)/shard_map/psum | solution.py:32
  121.2 7.3 %slice_subtract_fusion.44 = (f32[1,2048]{1,0:T(1,128)S(1)}, f32[1,2048]{1,0:T(1,128)S(1)}, f32[1,2048]{1,0:T(1,128)S(1)}, f32[1,2048]{1,0:T(1,128)S(1)}, f32[1,2...) fusion(f32[32,2048]{1,0:T(8,128)S(1)} %copy.10, f32[]{:T(128)} %bitcast.9, ...), kind=kLoop, calls=%fused_computation.188 | loop fusion | flops 65536 | bytes 163880 | tf_op jit(solution)/shard_map/sub | solution.py:19
  128.5 17.4 %fusion.80 = (f32[1,2048]{1,0:T(1,128)S(1)}, f32[1,2048]{1,0:T(1,128)S(1)}, f32[1,2048]{1,0:T(1,128)S(1)}, f32[1,2048]{1,0:T(1,128)S(1)}) fusion(f32[1,2048]{1,0:T(1,128)S(1)} %get-tuple-element.45, f32[1,2048]{1,0:T(1,128)S(1)} %get-tuple-element.47, f32[1,2048]{1,0:T(1,128)S(1)} %get-tuple-element.49, f32[1,2048]{1,0:T(1,128)S(1)} %get-tuple-element.51, ...), kind=kLoop, calls=%fused_computation.164 | loop fusion | flops 129024 | bytes 163944 | tf_op jit(solution)/shard_map/max | solution.py:20
  146.3 7.3 %slice_subtract_fusion.38 = (f32[1,2048]{1,0:T(1,128)S(1)}, f32[1,2048]{1,0:T(1,128)S(1)}, f32[1,2048]{1,0:T(1,128)S(1)}, f32[1,2048]{1,0:T(1,128)S(1)}, f32[1,2...) fusion(f32[32,2048]{1,0:T(8,128)S(1)} %constant_dynamic-update-slice_fusion.3, ...), kind=kLoop, calls=%fused_computation.182 | loop fusion | flops 65536 | bytes 163880 | tf_op jit(solution)/shard_map/sub | solution.py:19
  153.6 17.4 %fusion.81 = (f32[1,2048]{1,0:T(1,128)S(1)}, f32[1,2048]{1,0:T(1,128)S(1)}, f32[1,2048]{1,0:T(1,128)S(1)}, f32[1,2048]{1,0:T(1,128)S(1)}) fusion(f32[1,2048]{1,0:T(1,128)S(1)} %get-tuple-element.33, f32[1,2048]{1,0:T(1,128)S(1)} %get-tuple-element.35, f32[1,2048]{1,0:T(1,128)S(1)} %get-tuple-element.37, f32[1,2048]{1,0:T(1,128)S(1)} %get-tuple-element.39, ...), kind=kLoop, calls=%fused_computation.165 | loop fusion | flops 129024 | bytes 163944 | tf_op jit(solution)/shard_map/max | solution.py:20
  171.3 7.4 %slice_subtract_fusion.32 = (f32[1,2048]{1,0:T(1,128)S(1)}, f32[1,2048]{1,0:T(1,128)S(1)}, f32[1,2048]{1,0:T(1,128)S(1)}, f32[1,2048]{1,0:T(1,128)S(1)}, f32[1,2...) fusion(f32[32,2048]{1,0:T(8,128)S(1)} %constant_dynamic-update-slice_fusion.2, ...), kind=kLoop, calls=%fused_computation.176 | loop fusion | flops 65536 | bytes 163880 | tf_op jit(solution)/shard_map/sub | solution.py:19
  178.7 17.4 %fusion.82 = (f32[1,2048]{1,0:T(1,128)S(1)}, f32[1,2048]{1,0:T(1,128)S(1)}, f32[1,2048]{1,0:T(1,128)S(1)}, f32[1,2048]{1,0:T(1,128)S(1)}) fusion(f32[1,2048]{1,0:T(1,128)S(1)} %get-tuple-element.21, f32[1,2048]{1,0:T(1,128)S(1)} %get-tuple-element.23, f32[1,2048]{1,0:T(1,128)S(1)} %get-tuple-element.25, f32[1,2048]{1,0:T(1,128)S(1)} %get-tuple-element.27, ...), kind=kLoop, calls=%fused_computation.166 | loop fusion | flops 129024 | bytes 163944 | tf_op jit(solution)/shard_map/max | solution.py:20
  196.4 7.4 %slice_subtract_fusion.26 = (f32[1,2048]{1,0:T(1,128)S(1)}, f32[1,2048]{1,0:T(1,128)S(1)}, f32[1,2048]{1,0:T(1,128)S(1)}, f32[1,2048]{1,0:T(1,128)S(1)}, f32[1,2...) fusion(f32[32,2048]{1,0:T(8,128)S(1)} %constant_dynamic-update-slice_fusion.1, ...), kind=kLoop, calls=%fused_computation.170 | loop fusion | flops 65536 | bytes 163880 | tf_op jit(solution)/shard_map/sub | solution.py:19
  203.9 17.3 %fusion.83 = (f32[1,2048]{1,0:T(1,128)S(1)}, f32[1,2048]{1,0:T(1,128)S(1)}, f32[1,2048]{1,0:T(1,128)S(1)}, f32[1,2048]{1,0:T(1,128)S(1)}) fusion(f32[1,2048]{1,0:T(1,128)S(1)} %get-tuple-element.9, f32[1,2048]{1,0:T(1,128)S(1)} %get-tuple-element.11, f32[1,2048]{1,0:T(1,128)S(1)} %get-tuple-element.13, f32[1,2048]{1,0:T(1,128)S(1)} %get-tuple-element.15, ...), kind=kLoop, calls=%fused_computation.167 | loop fusion | flops 129024 | bytes 163944 | tf_op jit(solution)/shard_map/max | solution.py:20
  221.3 0.6 constant_dynamic-update-slice_fusion
  (17 shorter events, 1.4 us)
Async XLA Ops:
  6.5 28.3 %copy-start.1 = (f32[32,256]{1,0:T(8,128)S(1)}, f32[32,256]{1,0:T(8,128)}, u32[]{:S(2)}) copy-start(f32[32,256]{1,0:T(8,128)} %param.4) | copy-start | bytes 98308
  6.5 114.6 %all-reduce.2.cloned.1.call-start = ((), (), s32[]{:S(2)}) async-start(), calls=%async_computation | async-start | bytes 524288 | tf_op jit(solution)/shard_map/psum | solution.py:32
  196.2 25.1 %copy-start = (f32[32,2048]{1,0:T(8,128)}, f32[32,2048]{1,0:T(8,128)S(1)}, u32[]{:S(2)}) copy-start(f32[32,2048]{1,0:T(8,128)S(1)} %constant_dynamic-update-slice_fusion.1) | copy-start | bytes 786436
Sparse Core Ops, SparseCore 0:
  34.9 86.2 all-reduce.1
where the time goes:
time: 231 us; the launch traced here: 229 us
  other arithmetic  98.8 us (43%)
  blocking collectives  82.6 us (36%)
  matrix products  14.9 us (6%)
  between operations  13.5 us (6%)
  waiting for transfers between devices  10.5 us (5%)
  local copies, waits for them, and re-layouts  8.47 us (4%)
    max x4, other arithmetic, sweep(): fresh = jnp.maximum(olds[inner] + (cross[k] - total) / gram[k, k], 0.0)  69.4 us
    psum x1, blocking collectives, shards(): gram = lax.psum(own_gram, ('prow', 'pcol'))  69.1 us
    sub x4, other arithmetic, sweep(): total = total + gram[k, first + prior] * (fresh_rows[prior] - olds[prior])  29.4 us
    dot_general x1, matrix products, shards(): jnp.dot(lax.all_gather(w_trans, 'pcol', axis=1, tiled=True), data, precis...  13.8 us
    all_gather x1, blocking collectives, shards(): lax.all_gather(w_trans, 'pcol', axis=1, tiled=True)  13.5 us
    psum x1, waiting for transfers between devices, shards(): cross = lax.psum(cross_part, 'prow')  10.4 us
    slice x8, local copies, waits for them, and re-layouts, sweep(): total = total + gram[k, first + prior] * (fresh_rows[prior] - olds[prior])  5.72 us
  transfers between devices with their start and end apart: 1, of which 1 were waited for; matrix products, arithmetic and copies ran while one was open for 3% of the time, Pallas kernels for 0%

commit v1 on v0

v1 whole, which is shorter than its diff:
```python
import functools

import jax
import jax.numpy as jnp
from jax import lax
from jax.experimental import pallas as pl
from jax.experimental.pallas import tpu as pltpu
from jax.sharding import PartitionSpec as P

MESH = pl.DeviceIdType.MESH
F32 = jnp.float32
BF16 = jnp.bfloat16
HIGHEST = lax.Precision.HIGHEST
EARLY = 6
TILE = 256


def pieces(x, n):
    parts = []
    for i in range(n):
        top = x.astype(BF16)
        parts.append(top)
        if i < n - 1:
            x = x - top.astype(F32)
    return parts


def stacked(w):
    return jnp.concatenate(pieces(w, 3), axis=0)


def product(ws, d):
    both = jnp.concatenate(pieces(d, 2), axis=0)
    out = jnp.dot(jnp.concatenate([ws, ws], axis=1), both, preferred_element_type=F32)
    rank = out.shape[0] // 3
    return out[:rank] + (out[rank : 2 * rank] + out[2 * rank :])


def kernel(
    n_r, n_c, w_hbm, d_hbm, h_hbm, out_ref,
    wall, dbuf, wlate, acc, outbox, inbox, gout, gin, hold, hnew, spread,
    wsem, hsem, dsem, wsend, wrecv, gsend, grecv, psend, precv, osend, orecv,
):
    r, c = lax.axis_index("prow"), lax.axis_index("pcol")
    rank, depth = w_hbm.shape
    width = out_ref.shape[1] // n_r
    n_x = n_c // 2
    x, core = c // 2, c % 2

    def source(i):
        j = i // 2
        step = ((j + 1) // 2) * (2 * (j % 2) - 1)
        return ((x + step + n_x) % n_x) * 2 + (core + i) % 2

    def rows_copy(i):
        s = source(i)
        at = pl.ds(pl.multiple_of(s * depth, depth), depth)
        return pltpu.make_async_copy(d_hbm.at[at], dbuf.at[at], dsem.at[s])

    own_w = pltpu.make_async_copy(w_hbm, wall.at[c], wsem)
    own_w.start()
    rows_copy(0).start()

    barrier = pltpu.get_barrier_semaphore()
    for i in range(1, n_c):
        pl.semaphore_signal(barrier, inc=1, device_id=(r, (c + i) % n_c), device_id_type=MESH)
    for i in range(1, n_r):
        pl.semaphore_signal(barrier, inc=1, device_id=((r + i) % n_r, c), device_id_type=MESH)

    for i in range(1, n_c):
        rows_copy(i).start()
    own_cols = pl.ds(pl.multiple_of(r * width, width), width)
    own_h = pltpu.make_async_copy(h_hbm.at[:, own_cols], hold, hsem)
    own_h.start()
    own_w.wait()
    pl.semaphore_wait(barrier, n_c + n_r - 2)

    def w_copy(i, slot):
        return pltpu.make_async_remote_copy(
            src_ref=wall.at[c], dst_ref=wall.at[slot], send_sem=wsend.at[i], recv_sem=wrecv.at[slot],
            device_id=(r, source(i)), device_id_type=MESH,
        )

    for i in range(1, n_c):
        w_copy(i, c).start()

    acc[...] = jnp.zeros_like(acc)

    def early(i, _):
        s = source(i)

        @pl.when(i > 0)
        def _():
            w_copy(i, s).wait_recv()

        rows_copy(i).wait()
        ws = stacked(wall[s])
        at = pl.ds(pl.multiple_of(s * depth, depth), depth)
        for n in range(4):
            cols = pl.ds(n * 512, 512)
            acc[:, cols] += product(ws, dbuf[at, cols])
        return 0

    lax.fori_loop(0, EARLY, early, 0)

    for j in range(n_c - EARLY):
        s = source(EARLY + j)
        w_copy(EARLY + j, s).wait_recv()
        wlate[:, j * depth : (j + 1) * depth] = stacked(wall[s])

    def gram_step(i, g):
        w = wall[i]
        return g + lax.dot_general(w, w, (((1,), (1,)), ((), ())), precision=HIGHEST, preferred_element_type=F32)

    gram = lax.fori_loop(0, n_c, gram_step, jnp.zeros((rank, rank), F32))
    gout[...] = jnp.concatenate([gram[8 * i : 8 * i + 8] for i in range(rank // 8)], axis=1)
    gin[r] = gout[...]

    def g_copy(i, slot):
        return pltpu.make_async_remote_copy(
            src_ref=gout, dst_ref=gin.at[slot], send_sem=gsend.at[i], recv_sem=grecv.at[slot],
            device_id=((r + i) % n_r, c), device_id_type=MESH,
        )

    for i in range(1, n_r):
        g_copy(i, r).start()

    for j in range(n_c - EARLY):
        rows_copy(EARLY + j).wait()

    def p_copy(owner, slot):
        return pltpu.make_async_remote_copy(
            src_ref=outbox.at[owner], dst_ref=inbox.at[slot], send_sem=psend.at[owner], recv_sem=precv.at[slot],
            device_id=(owner, c), device_id_type=MESH,
        )

    n_tiles = out_ref.shape[1] // TILE
    per = TILE // width

    def late(i, _):
        t = (r // per + 1 + i) % n_tiles
        cols = pl.ds(pl.multiple_of(t * TILE, TILE), TILE)
        total = acc[:, cols]
        for j in range(n_c - EARLY):
            at = pl.ds(pl.multiple_of(source(EARLY + j) * depth, depth), depth)
            total = total + product(wlate[:, j * depth : (j + 1) * depth], dbuf[at, cols])
        for p in range(per):
            owner = t * per + p
            outbox[owner] = total[:, p * width : (p + 1) * width]

            @pl.when(owner != r)
            def _():
                p_copy(owner, r).start()

        return 0

    lax.fori_loop(0, n_tiles, late, 0)
    inbox[r] = outbox[r]

    def g_wait(i, _):
        g_copy(i, (r + i) % n_r).wait_recv()
        return 0

    lax.fori_loop(1, n_r, g_wait, 0)
    packed = gin[0]
    for i in range(1, n_r):
        packed = packed + gin[i]

    own_h.wait()
    lanes = lax.broadcasted_iota(jnp.int32, (8, 128), 1)
    subs = lax.broadcasted_iota(jnp.int32, (8, 128), 0)
    blocks = rank // 8
    inverse = []
    for b in range(blocks):
        diagonal = jnp.sum(jnp.where(lanes == rank * b + 8 * b + subs, packed, 0.0), axis=1, keepdims=True)
        inverse.append(jnp.broadcast_to(1.0 / diagonal, (8, width)))
    above = [jnp.zeros((8, width), F32) for _ in range(blocks)]
    for k in range(rank):
        old = jnp.broadcast_to(hold[k : k + 1, :], (8, width))
        for b in range(blocks):
            column = jnp.broadcast_to(packed[:, rank * b + k : rank * b + k + 1], (8, width)) * inverse[b]
            if 8 * b < k:
                masked = column if 8 * b + 8 <= k else jnp.where(subs < k - 8 * b, column, 0.0)
                above[b] = above[b] + masked * old
            if 8 * b + 7 > k:
                masked = column if 8 * b > k else jnp.where(subs > k - 8 * b, column, 0.0)
                spread[k, 8 * b : 8 * b + 8] = masked

    def p_wait(i, _):
        s = (r + i) % n_r
        p_copy(s, s).wait_recv()
        return 0

    lax.fori_loop(1, n_r, p_wait, 0)
    cross = inbox[0]
    for i in range(1, n_r):
        cross = cross + inbox[i]
    u = [cross[8 * b : 8 * b + 8] * inverse[b] - above[b] for b in range(blocks)]
    for k in range(rank):
        b0, s0 = k // 8, k % 8
        fresh = jnp.broadcast_to(jnp.maximum(u[b0][s0 : s0 + 1], 0.0), (8, width))
        for b in range(b0, blocks):
            if 8 * b + 7 > k:
                u[b] = u[b] - spread[k, 8 * b : 8 * b + 8] * fresh
    fresh = jnp.maximum(jnp.concatenate(u, axis=0), 0.0)
    hnew[...] = fresh
    out_ref[:, own_cols] = fresh

    def o_copy(i, slot):
        cols = pl.ds(pl.multiple_of(slot * width, width), width)
        return pltpu.make_async_remote_copy(
            src_ref=hnew, dst_ref=out_ref.at[:, cols], send_sem=osend.at[i], recv_sem=orecv.at[slot],
            device_id=((r + i) % n_r, c), device_id_type=MESH,
        )

    for i in range(1, n_r):
        o_copy(i, r).start()

    def finish(i, _):
        g_copy(i, r).wait_send()
        p_copy((r + i) % n_r, r).wait_send()
        o_copy(i, r).wait_send()
        o_copy(i, (r + i) % n_r).wait_recv()
        return 0

    lax.fori_loop(1, n_r, finish, 0)
    for i in range(1, n_c):
        w_copy(i, c).wait_send()


def solution(mesh):
    n_r, n_c = mesh.shape["prow"], mesh.shape["pcol"]

    def shards(data, w_trans, h_prior):
        rank, depth = w_trans.shape
        rows, cols = data.shape
        width = cols // n_r
        dma = pltpu.SemaphoreType.DMA
        return pl.pallas_call(
            functools.partial(kernel, n_r, n_c),
            out_shape=jax.ShapeDtypeStruct((rank, cols), F32),
            in_specs=[pl.BlockSpec(memory_space=pl.ANY)] * 3,
            out_specs=pl.BlockSpec(memory_space=pltpu.VMEM),
            scratch_shapes=[
                pltpu.VMEM((n_c, rank, depth), F32),
                pltpu.VMEM((rows, cols), F32),
                pltpu.VMEM((3 * rank, (n_c - EARLY) * depth), BF16),
                pltpu.VMEM((rank, cols), F32),
                pltpu.VMEM((n_r, rank, width), F32),
                pltpu.VMEM((n_r, rank, width), F32),
                pltpu.VMEM((8, rank * rank // 8), F32),
                pltpu.VMEM((n_r, 8, rank * rank // 8), F32),
                pltpu.VMEM((rank, width), F32),
                pltpu.VMEM((rank, width), F32),
                pltpu.VMEM((rank, rank, width), F32),
                dma, dma, dma((n_c,)),
                dma((n_c,)), dma((n_c,)),
                dma((n_r,)), dma((n_r,)),
                dma((n_r,)), dma((n_r,)),
                dma((n_r,)), dma((n_r,)),
            ],
            compiler_params=pltpu.CompilerParams(
                collective_id=0, has_side_effects=True, vmem_limit_bytes=40 * 2**20
            ),
            cost_estimate=pl.CostEstimate(
                flops=2 * rank * rows * cols, bytes_accessed=4 * rows * cols, transcendentals=0
            ),
        )(*(pltpu.with_memory_space_constraint(a, pltpu.HBM) for a in (w_trans, data, h_prior)))

    placed = (P("prow", "pcol"), P(None, ("prow", "pcol")), P(None, "pcol"))
    return jax.shard_map(shards, mesh=mesh, in_specs=placed, out_specs=P(None, "pcol"), check_vma=False)
```

time: 231 us -> 28.6 us (0.12)
  other arithmetic: 98.8 us -> 0 us
  blocking collectives: 82.6 us -> 0 us
  Pallas kernels: 0 us -> 27.8 us
  matrix products: 14.9 us -> 0 us
  between operations: 13.5 us -> 0.01 us
  waiting for transfers between devices: 10.5 us -> 0 us
  local copies, waits for them, and re-layouts: 8.47 us -> 0.71 us
    max x4 -> x0, other arithmetic: 69.4 us -> none  [sweep(): fresh = jnp.maximum(olds[inner] + (cross[k] - total) / gram[k, k], 0.0)]
    psum x1 -> x0, blocking collectives: 69.1 us -> none  [shards(): gram = lax.psum(own_gram, ('prow', 'pcol'))]
    sub x4 -> x0, other arithmetic: 29.4 us -> none  [sweep(): total = total + gram[k, first + prior] * (fresh_rows[prior] - olds[prior])]
    pallas_call x0 -> x1, Pallas kernels: none -> 27.8 us  [shards(): pl.pallas_call(functools.partial(kernel, n_r, n_c), out_shape=jax.ShapeDt...]
    dot_general x6 -> x0, matrix products: 14.9 us -> none  [the longest x1 13.8 us: shards(): jnp.dot(lax.all_gather(w_trans, 'pcol', axis=1, tiled=True), data, precis...]
    all_gather x1 -> x0, blocking collectives: 13.5 us -> none  [shards(): lax.all_gather(w_trans, 'pcol', axis=1, tiled=True)]
    psum x1 -> x0, waiting for transfers between devices: 10.4 us -> none  [shards(): cross = lax.psum(cross_part, 'prow')]
    slice x9 -> x0, local copies, waits for them, and re-layouts: 6.41 us -> none  [the longest x8 5.72 us: sweep(): total = total + gram[k, first + prior] * (fresh_rows[prior] - olds[prior])]
  transfers between devices with their start and end apart: 1 -> 0, of which waited for: 1 -> 0; matrix products, arithmetic and copies ran while one was open for 3% -> 0% of each run, Pallas kernels for 0% -> 0%
where the time goes in v1:
time: 28.6 us; the launch traced here: 28.5 us
  Pallas kernels  27.8 us (97%)
  local copies, waits for them, and re-layouts  0.71 us (2%)
    pallas_call x1, Pallas kernels, shards(): pl.pallas_call(functools.partial(kernel, n_r, n_c), out_shape=jax.ShapeDt...  27.8 us
    unnamed x1, local copies, waits for them, and re-layouts  0.71 us

profile of v1, /device:TPU:0, one launch (start us, length us, event | category | flops | bytes accessed | tf_op | source)
XLA Modules:
  0.0 28.5 jit_solution(7131180600066017661)
XLA Ops:
  0.0 27.8 %shard_map.37 = f32[32,2048]{1,0:T(8,128)S(1)} custom-call(f32[32,256]{1,0:T(8,128)} %w_hbm.1, f32[2048,2048]{1,0:T(8,128)} %d_hbm.1, f32[32,2048]{1,0:T(8,128)} %h_hbm.1), custom_call_target="tpu_custom_call" | custom-call | flops 268435456 | bytes 16777216 | tf_op jit(solution)/shard_map/pallas_call | solution.py:239
  27.8 0.7 %copy.5 = f32[32,2048]{1,0:T(8,128)} copy(f32[32,2048]{1,0:T(8,128)S(1)} %shard_map.37) | data formatting | bytes 524288

commit v2 on v1

v2 whole, which is shorter than its diff:
```python
import functools

import jax
import jax.numpy as jnp
from jax import lax
from jax.experimental import pallas as pl
from jax.experimental.pallas import tpu as pltpu
from jax.sharding import PartitionSpec as P

MESH = pl.DeviceIdType.MESH
F32 = jnp.float32
BF16 = jnp.bfloat16
EARLY = 6
TILE = 256


def pieces(x, n):
    parts = []
    for i in range(n):
        top = x.astype(BF16)
        parts.append(top)
        if i < n - 1:
            x = x - top.astype(F32)
    return parts


def stacked(w):
    return jnp.concatenate(pieces(w, 3), axis=0)


def product(ws, d):
    both = jnp.concatenate(pieces(d, 2), axis=0)
    out = jnp.dot(jnp.concatenate([ws, ws], axis=1), both, preferred_element_type=F32)
    rank = out.shape[0] // 3
    return out[:rank] + (out[rank : 2 * rank] + out[2 * rank :])


def moments(ws):
    return lax.dot_general(ws, ws, (((1,), (1,)), ((), ())), preferred_element_type=F32)


def packed_gram(m):
    rank = m.shape[0] // 3
    m = m[:rank] + (m[rank : 2 * rank] + m[2 * rank :])
    m = m[:, :rank] + (m[:, rank : 2 * rank] + m[:, 2 * rank :])
    return jnp.concatenate([m[8 * b : 8 * b + 8] for b in range(rank // 8)], axis=1)


def kernel(
    n_r, n_c, w_hbm, d_hbm, h_hbm, out_ref,
    wall, dbuf, wlate, acc, mom, outbox, inbox, hold, hnew,
    wsem, hsem, dsem, greet, wsend, wrecv, psend, precv, osend, orecv,
):
    r, c = lax.axis_index("prow"), lax.axis_index("pcol")
    rank, depth = w_hbm.shape
    width = out_ref.shape[1] // n_r
    n_x = n_c // 2
    x, core = c // 2, c % 2

    def source(i):
        j = i // 2
        step = ((j + 1) // 2) * (2 * (j % 2) - 1)
        return ((x + step + n_x) % n_x) * 2 + (core + i) % 2

    def rows_copy(i):
        s = source(i)
        at = pl.ds(pl.multiple_of(s * depth, depth), depth)
        return pltpu.make_async_copy(d_hbm.at[at], dbuf.at[at], dsem.at[s])

    own_w = pltpu.make_async_copy(w_hbm, wall.at[c], wsem)
    own_w.start()
    barrier = pltpu.get_barrier_semaphore()
    for i in range(1, n_c):
        pl.semaphore_signal(barrier, inc=1, device_id=(r, source(i)), device_id_type=MESH)
    z, y = r // LINE, r % LINE
    n_z = n_r // LINE
    for i in range(1, LINE):
        pl.semaphore_signal(barrier, inc=1, device_id=(z * LINE + (y + i) % LINE, c), device_id_type=MESH)
    for i in range(1, n_z):
        pl.semaphore_signal(barrier, inc=1, device_id=((z + i) % n_z * LINE + y, c), device_id_type=MESH)

    for i in range(n_c):
        rows_copy(i).start()
    own_cols = pl.ds(pl.multiple_of(r * width, width), width)
    own_h = pltpu.make_async_copy(h_hbm.at[:, own_cols], hold, hsem)
    own_h.start()
    own_w.wait()
    pl.semaphore_wait(barrier, n_c + LINE + n_z - 3)

    def w_copy(i, slot):
        return pltpu.make_async_remote_copy(
            src_ref=wall.at[c], dst_ref=wall.at[slot], send_sem=wsend.at[i], recv_sem=wrecv.at[slot],
            device_id=(r, source(i)), device_id_type=MESH,
        )

    for i in (1, 6, 7, 2, 4, 3, 5):
        w_copy(i, c).start()
    for i in range(1, n_z):
        pl.semaphore_signal(greet, inc=1, device_id=((z + i) % n_z * LINE + y, c), device_id_type=MESH)

    acc[...] = jnp.zeros_like(acc)
    mom[...] = jnp.zeros_like(mom)

    def early(i, _):
        s = source(i)

        @pl.when(i > 0)
        def _():
            w_copy(i, s).wait_recv()

        rows_copy(i).wait()
        ws = stacked(wall[s])
        at = pl.ds(pl.multiple_of(s * depth, depth), depth)
        for n in range(4):
            cols = pl.ds(n * 512, 512)
            acc[:, cols] += product(ws, dbuf[at, cols])
        mom[...] += moments(ws)
        return 0

    lax.fori_loop(0, EARLY, early, 0)
    pl.semaphore_wait(greet, n_z - 1)
    for j in range(EARLY, n_c):
        rows_copy(j).wait()

    for j in range(n_c - EARLY):
        s = source(EARLY + j)
        w_copy(EARLY + j, s).wait_recv()
        wlate[:, j * depth : (j + 1) * depth] = stacked(wall[s])
    gram = packed_gram(mom[...] + moments(wlate[...]))
    for i in range(n_r):
        outbox[i, rank:] = gram

    def p_copy(owner, slot):
        return pltpu.make_async_remote_copy(
            src_ref=outbox.at[owner], dst_ref=inbox.at[slot], send_sem=psend.at[owner], recv_sem=precv.at[slot],
            device_id=(owner, c), device_id_type=MESH,
        )

    n_tiles = out_ref.shape[1] // TILE
    per = TILE // width

    def late(i, _):
        t = (r // per + n_tiles // 2 + 1 + i) % n_tiles
        cols = pl.ds(pl.multiple_of(t * TILE, TILE), TILE)
        total = acc[:, cols]
        for j in range(n_c - EARLY):
            at = pl.ds(pl.multiple_of(source(EARLY + j) * depth, depth), depth)
            total = total + product(wlate[:, j * depth : (j + 1) * depth], dbuf[at, cols])
        for p in range(per):
            owner = t * per + p
            outbox[owner, :rank] = total[:, p * width : (p + 1) * width]

            @pl.when(owner != r)
            def _():
                p_copy(owner, r).start()

        return 0

    lax.fori_loop(0, n_tiles, late, 0)
    inbox[r] = outbox[r]

    own_h.wait()

    def p_wait(i, _):
        s = (r + i) % n_r
        p_copy(s, s).wait_recv()
        return 0

    lax.fori_loop(1, n_r, p_wait, 0)

    total = inbox[0]
    for i in range(1, n_r):
        total = total + inbox[i]
    packed = total[rank:]
    lanes = lax.broadcasted_iota(jnp.int32, packed.shape, 1)
    subs = lax.broadcasted_iota(jnp.int32, (8, width), 0)
    blocks = rank // 8
    inverse = []
    for b in range(blocks):
        diagonal = jnp.sum(jnp.where(lanes == rank * b + 8 * b + subs, packed, 0.0), axis=1, keepdims=True)
        inverse.append(jnp.broadcast_to(1.0 / diagonal, (8, width)))

    def column(b, k):
        return jnp.broadcast_to(packed[:, rank * b + k : rank * b + k + 1], (8, width)) * inverse[b]

    u = [total[8 * b : 8 * b + 8] * inverse[b] for b in range(blocks)]
    lower = {}
    for k in range(rank):
        b0, s0 = k // 8, k % 8
        old = jnp.broadcast_to(hold[k : k + 1, :], (8, width))
        for b in range(blocks):
            whole = column(b, k)
            if b < b0:
                u[b] = u[b] - whole * old
            elif b > b0:
                lower[k, b] = whole
            else:
                if s0:
                    u[b] = u[b] - jnp.where(subs < s0, whole, 0.0) * old
                if s0 < 7:
                    lower[k, b] = jnp.where(subs > s0, whole, 0.0)
    for k in range(rank):
        b0, s0 = k // 8, k % 8
        fresh = jnp.broadcast_to(jnp.maximum(u[b0][s0 : s0 + 1], 0.0), (8, width))
        for b in range(b0, blocks):
            if (k, b) in lower:
                u[b] = u[b] - lower[k, b] * fresh
    fresh = jnp.maximum(jnp.concatenate(u, axis=0), 0.0)
    hnew[...] = fresh

    def o_copy(i, slot):
        cols = pl.ds(pl.multiple_of(slot * width, width), width)
        return pltpu.make_async_remote_copy(
            src_ref=hnew, dst_ref=out_ref.at[:, cols], send_sem=osend.at[i], recv_sem=orecv.at[slot],
            device_id=(i, c), device_id_type=MESH,
        )

    for i in ORDER:
        @pl.when(i != r)
        def _():
            o_copy(i, r).start()

    out_ref[:, own_cols] = fresh

    def finish(i, _):
        s = (r + i) % n_r
        o_copy(s, s).wait_recv()
        p_copy(s, r).wait_send()
        o_copy(s, r).wait_send()
        return 0

    lax.fori_loop(1, n_r, finish, 0)
    for i in range(1, n_c):
        w_copy(i, c).wait_send()


LINE = 4
ORDER = (0, 1, 4, 5, 2, 3, 8, 6, 7, 9, 12, 10, 11, 13, 14, 15)


def solution(mesh):
    n_r, n_c = mesh.shape["prow"], mesh.shape["pcol"]

    def shards(data, w_trans, h_prior):
        rank, depth = w_trans.shape
        rows, cols = data.shape
        width = cols // n_r
        dma = pltpu.SemaphoreType.DMA
        return pl.pallas_call(
            functools.partial(kernel, n_r, n_c),
            out_shape=jax.ShapeDtypeStruct((rank, cols), F32),
            in_specs=[pl.BlockSpec(memory_space=pl.ANY)] * 3,
            out_specs=pl.BlockSpec(memory_space=pltpu.VMEM),
            scratch_shapes=[
                pltpu.VMEM((n_c, rank, depth), F32),
                pltpu.VMEM((rows, cols), F32),
                pltpu.VMEM((3 * rank, (n_c - EARLY) * depth), BF16),
                pltpu.VMEM((rank, cols), F32),
                pltpu.VMEM((3 * rank, 3 * rank), F32),
                pltpu.VMEM((n_r, rank + 8, width), F32),
                pltpu.VMEM((n_r, rank + 8, width), F32),
                pltpu.VMEM((rank, width), F32),
                pltpu.VMEM((rank, width), F32),
                dma, dma, dma((n_c,)), pltpu.SemaphoreType.REGULAR,
                dma((n_c,)), dma((n_c,)),
                dma((n_r,)), dma((n_r,)),
                dma((n_r,)), dma((n_r,)),
            ],
            compiler_params=pltpu.CompilerParams(
                collective_id=0, has_side_effects=True, vmem_limit_bytes=40 * 2**20
            ),
            cost_estimate=pl.CostEstimate(
                flops=2 * rank * rows * cols, bytes_accessed=4 * rows * cols, transcendentals=0
            ),
        )(*(pltpu.with_memory_space_constraint(a, pltpu.HBM) for a in (w_trans, data, h_prior)))

    placed = (P("prow", "pcol"), P(None, ("prow", "pcol")), P(None, "pcol"))
    return jax.shard_map(shards, mesh=mesh, in_specs=placed, out_specs=P(None, "pcol"), check_vma=False)
```

time: 28.6 us -> 26.6 us (0.930)
  Pallas kernels: 27.8 us -> 25.7 us
    pallas_call x1, Pallas kernels: 27.8 us -> 25.7 us  [shards(): pl.pallas_call(functools.partial(kernel, n_r, n_c), out_shape=jax.ShapeDt...]
where the time goes in v2:
time: 26.6 us; the launch traced here: 26.5 us
  Pallas kernels  25.7 us (97%)
  local copies, waits for them, and re-layouts  0.71 us (3%)
    pallas_call x1, Pallas kernels, shards(): pl.pallas_call(functools.partial(kernel, n_r, n_c), out_shape=jax.ShapeDt...  25.7 us
    unnamed x1, local copies, waits for them, and re-layouts  0.71 us

profile of v2, /device:TPU:0, one launch (start us, length us, event | category | flops | bytes accessed | tf_op | source)
XLA Modules:
  0.0 26.5 jit_solution(9820711096587607944)
XLA Ops:
  0.0 25.7 %shard_map.37 = f32[32,2048]{1,0:T(8,128)S(1)} custom-call(f32[32,256]{1,0:T(8,128)} %w_hbm.1, f32[2048,2048]{1,0:T(8,128)} %d_hbm.1, f32[32,2048]{1,0:T(8,128)} %h_hbm.1), custom_call_target="tpu_custom_call" | custom-call | flops 268435456 | bytes 16777216 | tf_op jit(solution)/shard_map/pallas_call | solution.py:249
  25.8 0.7 %copy.5 = f32[32,2048]{1,0:T(8,128)} copy(f32[32,2048]{1,0:T(8,128)S(1)} %shard_map.37) | data formatting | bytes 524288

commit v3 on v2

--- a/solution.py
+++ b/solution.py
@@ -62,10 +62,10 @@
         step = ((j + 1) // 2) * (2 * (j % 2) - 1)
         return ((x + step + n_x) % n_x) * 2 + (core + i) % 2
 
-    def rows_copy(i):
-        s = source(i)
-        at = pl.ds(pl.multiple_of(s * depth, depth), depth)
-        return pltpu.make_async_copy(d_hbm.at[at], dbuf.at[at], dsem.at[s])
+    def rows_copy(j):
+        chip = source(2 * j) // 2
+        at = pl.ds(pl.multiple_of(chip * 2 * depth, 2 * depth), 2 * depth)
+        return pltpu.make_async_copy(d_hbm.at[at], dbuf.at[at], dsem.at[j])
 
     own_w = pltpu.make_async_copy(w_hbm, wall.at[c], wsem)
     own_w.start()
@@ -79,8 +79,8 @@
     for i in range(1, n_z):
         pl.semaphore_signal(barrier, inc=1, device_id=((z + i) % n_z * LINE + y, c), device_id_type=MESH)
 
-    for i in range(n_c):
-        rows_copy(i).start()
+    for j in range(n_x):
+        rows_copy(j).start()
     own_cols = pl.ds(pl.multiple_of(r * width, width), width)
     own_h = pltpu.make_async_copy(h_hbm.at[:, own_cols], hold, hsem)
     own_h.start()
@@ -108,7 +108,10 @@
         def _():
             w_copy(i, s).wait_recv()
 
-        rows_copy(i).wait()
+        @pl.when(i % 2 == 0)
+        def _():
+            rows_copy(i // 2).wait()
+
         ws = stacked(wall[s])
         at = pl.ds(pl.multiple_of(s * depth, depth), depth)
         for n in range(4):
@@ -119,7 +122,7 @@
 
     lax.fori_loop(0, EARLY, early, 0)
     pl.semaphore_wait(greet, n_z - 1)
-    for j in range(EARLY, n_c):
+    for j in range(EARLY // 2, n_x):
         rows_copy(j).wait()
 
     for j in range(n_c - EARLY):
@@ -132,7 +135,7 @@
 
     def p_copy(owner, slot):
         return pltpu.make_async_remote_copy(
-            src_ref=outbox.at[owner], dst_ref=inbox.at[slot], send_sem=psend.at[owner], recv_sem=precv.at[slot],
+            src_ref=outbox.at[owner], dst_ref=inbox.at[slot], send_sem=psend, recv_sem=precv,
             device_id=(owner, c), device_id_type=MESH,
         )
 
@@ -140,7 +143,7 @@
     per = TILE // width
 
     def late(i, _):
-        t = (r // per + n_tiles // 2 + 1 + i) % n_tiles
+        t = (r // per + lax.shift_right_logical(FAR_FIRST, 4 * i) % 8) % n_tiles
         cols = pl.ds(pl.multiple_of(t * TILE, TILE), TILE)
         total = acc[:, cols]
         for j in range(n_c - EARLY):
@@ -161,12 +164,8 @@
 
     own_h.wait()
 
-    def p_wait(i, _):
-        s = (r + i) % n_r
-        p_copy(s, s).wait_recv()
-        return 0
-
-    lax.fori_loop(1, n_r, p_wait, 0)
+    all_partials = pltpu.make_async_copy(outbox.at[1:], inbox.at[1:], precv)
+    all_partials.wait()
 
     total = inbox[0]
     for i in range(1, n_r):
@@ -211,7 +210,7 @@
     def o_copy(i, slot):
         cols = pl.ds(pl.multiple_of(slot * width, width), width)
         return pltpu.make_async_remote_copy(
-            src_ref=hnew, dst_ref=out_ref.at[:, cols], send_sem=osend.at[i], recv_sem=orecv.at[slot],
+            src_ref=hnew, dst_ref=out_ref.at[:, cols], send_sem=osend, recv_sem=orecv,
             device_id=(i, c), device_id_type=MESH,
         )
 
@@ -222,20 +221,17 @@
 
     out_ref[:, own_cols] = fresh
 
-    def finish(i, _):
-        s = (r + i) % n_r
-        o_copy(s, s).wait_recv()
-        p_copy(s, r).wait_send()
-        o_copy(s, r).wait_send()
-        return 0
-
-    lax.fori_loop(1, n_r, finish, 0)
     for i in range(1, n_c):
         w_copy(i, c).wait_send()
+    pltpu.make_async_copy(outbox.at[1:], inbox.at[1:], psend).wait()
+    others = pl.ds(0, (n_r - 1) * width)
+    pltpu.make_async_copy(out_ref.at[:, others], out_ref.at[:, others], osend).wait()
+    pltpu.make_async_copy(out_ref.at[:, others], out_ref.at[:, others], orecv).wait()
 
 
 LINE = 4
-ORDER = (0, 1, 4, 5, 2, 3, 8, 6, 7, 9, 12, 10, 11, 13, 14, 15)
+FAR_FIRST = 0x01627345
+ORDER = (0, 4, 1, 3, 2, 5, 7, 6, 8, 9, 11, 10, 12, 13, 15, 14)
 
 
 def solution(mesh):
@@ -261,10 +257,9 @@
                 pltpu.VMEM((n_r, rank + 8, width), F32),
                 pltpu.VMEM((rank, width), F32),
                 pltpu.VMEM((rank, width), F32),
-                dma, dma, dma((n_c,)), pltpu.SemaphoreType.REGULAR,
+                dma, dma, dma((n_c // 2,)), pltpu.SemaphoreType.REGULAR,
                 dma((n_c,)), dma((n_c,)),
-                dma((n_r,)), dma((n_r,)),
-                dma((n_r,)), dma((n_r,)),
+                dma, dma, dma, dma,
             ],
             compiler_params=pltpu.CompilerParams(
                 collective_id=0, has_side_effects=True, vmem_limit_bytes=40 * 2**20

time: 26.6 us -> 26 us (0.977)
  Pallas kernels: 25.7 us -> 25.2 us
    pallas_call x1, Pallas kernels: 25.7 us -> 25.2 us  [shards(): pl.pallas_call(functools.partial(kernel, n_r, n_c), out_shape=jax.ShapeDt...]
where the time goes in v3:
time: 26 us; the launch traced here: 25.9 us
  Pallas kernels  25.2 us (97%)
  local copies, waits for them, and re-layouts  0.71 us (3%)
    pallas_call x1, Pallas kernels, shards(): pl.pallas_call(functools.partial(kernel, n_r, n_c), out_shape=jax.ShapeDt...  25.2 us
    unnamed x1, local copies, waits for them, and re-layouts  0.71 us

profile of v3, /device:TPU:0, one launch (start us, length us, event | category | flops | bytes accessed | tf_op | source)
XLA Modules:
  0.0 25.9 jit_solution(10964137586456819871)
XLA Ops:
  0.0 25.2 %shard_map.37 = f32[32,2048]{1,0:T(8,128)S(1)} custom-call(f32[32,256]{1,0:T(8,128)} %w_hbm.1, f32[2048,2048]{1,0:T(8,128)} %d_hbm.1, f32[32,2048]{1,0:T(8,128)} %h_hbm.1), custom_call_target="tpu_custom_call" | custom-call | flops 268435456 | bytes 16777216 | tf_op jit(solution)/shard_map/pallas_call | solution.py:245
  25.2 0.7 %copy.5 = f32[32,2048]{1,0:T(8,128)} copy(f32[32,2048]{1,0:T(8,128)S(1)} %shard_map.37) | data formatting | bytes 524288

commit v4 on v3

--- a/solution.py
+++ b/solution.py
@@ -11,7 +11,6 @@
 F32 = jnp.float32
 BF16 = jnp.bfloat16
 EARLY = 6
-TILE = 256
 
 
 def pieces(x, n):
@@ -48,8 +47,8 @@
 
 def kernel(
     n_r, n_c, w_hbm, d_hbm, h_hbm, out_ref,
-    wall, dbuf, wlate, acc, mom, outbox, inbox, hold, hnew,
-    wsem, hsem, dsem, greet, wsend, wrecv, psend, precv, osend, orecv,
+    wall, dbuf, wlate, acc, gout, gin, grow, outbox, inbox, hold, spread, hnew,
+    wsem, hsem, dsem, greet, wsend, wrecv, gsend, grecv, rsend, rrecv, psend, precv, osend, orecv,
 ):
     r, c = lax.axis_index("prow"), lax.axis_index("pcol")
     rank, depth = w_hbm.shape
@@ -93,16 +92,29 @@
             device_id=(r, source(i)), device_id_type=MESH,
         )
 
-    for i in (1, 6, 7, 2, 4, 3, 5):
+    for i in (1, 2, 4, 3, 5, 6, 7):
         w_copy(i, c).start()
     for i in range(1, n_z):
         pl.semaphore_signal(greet, inc=1, device_id=((z + i) % n_z * LINE + y, c), device_id_type=MESH)
 
     acc[...] = jnp.zeros_like(acc)
-    mom[...] = jnp.zeros_like(mom)
+    gout[...] = packed_gram(moments(stacked(wall[c])))
+    gin[r] = gout[...]
+
+    def g_copy(i):
+        return pltpu.make_async_remote_copy(
+            src_ref=gout, dst_ref=gin.at[r], send_sem=gsend, recv_sem=grecv,
+            device_id=((r + i) % n_r, c), device_id_type=MESH,
+        )
 
     def early(i, _):
         s = source(i)
+
+        @pl.when(i == 2)
+        def _():
+            pl.semaphore_wait(greet, n_z - 1)
+            for k in range(1, n_r):
+                g_copy(k).start()
 
         @pl.when(i > 0)
         def _():
@@ -117,21 +129,17 @@
         for n in range(4):
             cols = pl.ds(n * 512, 512)
             acc[:, cols] += product(ws, dbuf[at, cols])
-        mom[...] += moments(ws)
         return 0
 
     lax.fori_loop(0, EARLY, early, 0)
-    pl.semaphore_wait(greet, n_z - 1)
     for j in range(EARLY // 2, n_x):
         rows_copy(j).wait()
 
-    for j in range(n_c - EARLY):
-        s = source(EARLY + j)
-        w_copy(EARLY + j, s).wait_recv()
+    chip = source(EARLY) // 2
+    for j in range(2):
+        s = 2 * chip + j
+        w_copy(EARLY, s).wait_recv()
         wlate[:, j * depth : (j + 1) * depth] = stacked(wall[s])
-    gram = packed_gram(mom[...] + moments(wlate[...]))
-    for i in range(n_r):
-        outbox[i, rank:] = gram
 
     def p_copy(owner, slot):
         return pltpu.make_async_remote_copy(
@@ -139,38 +147,39 @@
             device_id=(owner, c), device_id_type=MESH,
         )
 
-    n_tiles = out_ref.shape[1] // TILE
-    per = TILE // width
-
-    def late(i, _):
-        t = (r // per + lax.shift_right_logical(FAR_FIRST, 4 * i) % 8) % n_tiles
-        cols = pl.ds(pl.multiple_of(t * TILE, TILE), TILE)
-        total = acc[:, cols]
-        for j in range(n_c - EARLY):
-            at = pl.ds(pl.multiple_of(source(EARLY + j) * depth, depth), depth)
-            total = total + product(wlate[:, j * depth : (j + 1) * depth], dbuf[at, cols])
-        for p in range(per):
-            owner = t * per + p
-            outbox[owner, :rank] = total[:, p * width : (p + 1) * width]
-
-            @pl.when(owner != r)
-            def _():
-                p_copy(owner, r).start()
-
-        return 0
-
-    lax.fori_loop(0, n_tiles, late, 0)
+    both = wlate[...]
+    at = pl.ds(pl.multiple_of(source(EARLY) // 2 * 2 * depth, 2 * depth), 2 * depth)
+    for dz in (2, 1, 3, 0):
+        row = (z + dz) % n_z
+        cols = pl.ds(pl.multiple_of(row * LINE * width, LINE * width), LINE * width)
+        total = acc[:, cols] + product(both, dbuf[at, cols])
+        for p in range(LINE):
+            outbox[row * LINE + p] = total[:, p * width : (p + 1) * width]
+        for dy in (2, 1, 3, 0):
+            if dz or dy:
+                p_copy(row * LINE + (y + dy) % LINE, r).start()
     inbox[r] = outbox[r]
 
+    pltpu.make_async_copy(gin.at[1:], gin.at[1:], grecv).wait()
+    packed = gin[0]
+    for i in range(1, n_r):
+        packed = packed + gin[i]
+    grow[c] = packed
+
+    def r_copy(i):
+        return pltpu.make_async_remote_copy(
+            src_ref=grow.at[c], dst_ref=grow.at[c], send_sem=rsend, recv_sem=rrecv,
+            device_id=(r, source(i)), device_id_type=MESH,
+        )
+
+    for i in range(1, n_c):
+        r_copy(i).start()
     own_h.wait()
-
-    all_partials = pltpu.make_async_copy(outbox.at[1:], inbox.at[1:], precv)
-    all_partials.wait()
-
-    total = inbox[0]
-    for i in range(1, n_r):
-        total = total + inbox[i]
-    packed = total[rank:]
+    pltpu.make_async_copy(grow.at[1:], grow.at[1:], rrecv).wait()
+    packed = grow[0]
+    for i in range(1, n_c):
+        packed = packed + grow[i]
+
     lanes = lax.broadcasted_iota(jnp.int32, packed.shape, 1)
     subs = lax.broadcasted_iota(jnp.int32, (8, width), 0)
     blocks = rank // 8
@@ -182,28 +191,34 @@
     def column(b, k):
         return jnp.broadcast_to(packed[:, rank * b + k : rank * b + k + 1], (8, width)) * inverse[b]
 
-    u = [total[8 * b : 8 * b + 8] * inverse[b] for b in range(blocks)]
-    lower = {}
+    above = [jnp.zeros((8, width), F32) for _ in range(blocks)]
+    lower = set()
     for k in range(rank):
         b0, s0 = k // 8, k % 8
         old = jnp.broadcast_to(hold[k : k + 1, :], (8, width))
         for b in range(blocks):
             whole = column(b, k)
             if b < b0:
-                u[b] = u[b] - whole * old
-            elif b > b0:
-                lower[k, b] = whole
-            else:
-                if s0:
-                    u[b] = u[b] - jnp.where(subs < s0, whole, 0.0) * old
-                if s0 < 7:
-                    lower[k, b] = jnp.where(subs > s0, whole, 0.0)
+                above[b] = above[b] + whole * old
+            elif b == b0 and s0:
+                above[b] = above[b] + jnp.where(subs < s0, whole, 0.0) * old
+            if b > b0 or (b == b0 and s0 < 7):
+                spread[k, 8 * b : 8 * b + 8] = whole if b > b0 else jnp.where(subs > s0, whole, 0.0)
+                lower.add((k, b))
+
+    all_partials = pltpu.make_async_copy(outbox.at[1:], inbox.at[1:], precv)
+    all_partials.wait()
+
+    total = inbox[0]
+    for i in range(1, n_r):
+        total = total + inbox[i]
+    u = [total[8 * b : 8 * b + 8] * inverse[b] - above[b] for b in range(blocks)]
     for k in range(rank):
         b0, s0 = k // 8, k % 8
         fresh = jnp.broadcast_to(jnp.maximum(u[b0][s0 : s0 + 1], 0.0), (8, width))
         for b in range(b0, blocks):
             if (k, b) in lower:
-                u[b] = u[b] - lower[k, b] * fresh
+                u[b] = u[b] - spread[k, 8 * b : 8 * b + 8] * fresh
     fresh = jnp.maximum(jnp.concatenate(u, axis=0), 0.0)
     hnew[...] = fresh
 
@@ -223,6 +238,8 @@
 
     for i in range(1, n_c):
         w_copy(i, c).wait_send()
+    pltpu.make_async_copy(gin.at[1:], gin.at[1:], gsend).wait()
+    pltpu.make_async_copy(grow.at[1:], grow.at[1:], rsend).wait()
     pltpu.make_async_copy(outbox.at[1:], inbox.at[1:], psend).wait()
     others = pl.ds(0, (n_r - 1) * width)
     pltpu.make_async_copy(out_ref.at[:, others], out_ref.at[:, others], osend).wait()
@@ -230,7 +247,6 @@
 
 
 LINE = 4
-FAR_FIRST = 0x01627345
 ORDER = (0, 4, 1, 3, 2, 5, 7, 6, 8, 9, 11, 10, 12, 13, 15, 14)
 
 
@@ -252,13 +268,17 @@
                 pltpu.VMEM((rows, cols), F32),
                 pltpu.VMEM((3 * rank, (n_c - EARLY) * depth), BF16),
                 pltpu.VMEM((rank, cols), F32),
-                pltpu.VMEM((3 * rank, 3 * rank), F32),
-                pltpu.VMEM((n_r, rank + 8, width), F32),
-                pltpu.VMEM((n_r, rank + 8, width), F32),
+                pltpu.VMEM((8, rank * rank // 8), F32),
+                pltpu.VMEM((n_r, 8, rank * rank // 8), F32),
+                pltpu.VMEM((n_c, 8, rank * rank // 8), F32),
+                pltpu.VMEM((n_r, rank, width), F32),
+                pltpu.VMEM((n_r, rank, width), F32),
                 pltpu.VMEM((rank, width), F32),
+                pltpu.VMEM((rank, rank, width), F32),
                 pltpu.VMEM((rank, width), F32),
                 dma, dma, dma((n_c // 2,)), pltpu.SemaphoreType.REGULAR,
                 dma((n_c,)), dma((n_c,)),
+                dma, dma, dma, dma,
                 dma, dma, dma, dma,
             ],
             compiler_params=pltpu.CompilerParams(

time: 26 us -> 24.5 us (0.942)
  Pallas kernels: 25.2 us -> 23.7 us
    pallas_call x1, Pallas kernels: 25.2 us -> 23.7 us  [shards(): pl.pallas_call(functools.partial(kernel, n_r, n_c), out_shape=jax.ShapeDt...]
where the time goes in v4:
time: 24.5 us; the launch traced here: 24.4 us
  Pallas kernels  23.7 us (97%)
  local copies, waits for them, and re-layouts  0.71 us (3%)
    pallas_call x1, Pallas kernels, shards(): pl.pallas_call(functools.partial(kernel, n_r, n_c), out_shape=jax.ShapeDt...  23.7 us
    unnamed x1, local copies, waits for them, and re-layouts  0.71 us

profile of v4, /device:TPU:0, one launch (start us, length us, event | category | flops | bytes accessed | tf_op | source)
XLA Modules:
  0.0 24.4 jit_solution(16037268880789327669)
XLA Ops:
  0.0 23.7 %shard_map.37 = f32[32,2048]{1,0:T(8,128)S(1)} custom-call(f32[32,256]{1,0:T(8,128)} %w_hbm.1, f32[2048,2048]{1,0:T(8,128)} %d_hbm.1, f32[32,2048]{1,0:T(8,128)} %h_hbm.1), custom_call_target="tpu_custom_call" | custom-call | flops 268435456 | bytes 16777216 | tf_op jit(solution)/shard_map/pallas_call | solution.py:261
  23.7 0.7 %copy.5 = f32[32,2048]{1,0:T(8,128)} copy(f32[32,2048]{1,0:T(8,128)S(1)} %shard_map.37) | data formatting | bytes 524288

commit v5 on v4

--- a/solution.py
+++ b/solution.py
@@ -92,7 +92,7 @@
             device_id=(r, source(i)), device_id_type=MESH,
         )
 
-    for i in (1, 2, 4, 3, 5, 6, 7):
+    for i in range(1, n_c):
         w_copy(i, c).start()
     for i in range(1, n_z):
         pl.semaphore_signal(greet, inc=1, device_id=((z + i) % n_z * LINE + y, c), device_id_type=MESH)
@@ -147,17 +147,27 @@
             device_id=(owner, c), device_id_type=MESH,
         )
 
-    both = wlate[...]
     at = pl.ds(pl.multiple_of(source(EARLY) // 2 * 2 * depth, 2 * depth), 2 * depth)
-    for dz in (2, 1, 3, 0):
-        row = (z + dz) % n_z
+    def late(i, _):
+        row = lax.shift_right_logical(FAR_FIRST, 4 * i) % 8
         cols = pl.ds(pl.multiple_of(row * LINE * width, LINE * width), LINE * width)
-        total = acc[:, cols] + product(both, dbuf[at, cols])
+        total = acc[:, cols] + product(wlate[...], dbuf[at, cols])
         for p in range(LINE):
             outbox[row * LINE + p] = total[:, p * width : (p + 1) * width]
-        for dy in (2, 1, 3, 0):
-            if dz or dy:
-                p_copy(row * LINE + (y + dy) % LINE, r).start()
+
+        def send(k, _):
+            piece = row * LINE + (y + lax.shift_right_logical(FAR_FIRST, 4 * k) % 8) % LINE
+
+            @pl.when(piece != r)
+            def _():
+                p_copy(piece, r).start()
+
+            return 0
+
+        lax.fori_loop(0, LINE, send, 0)
+        return 0
+
+    lax.fori_loop(0, n_z, late, 0)
     inbox[r] = outbox[r]
 
     pltpu.make_async_copy(gin.at[1:], gin.at[1:], grecv).wait()
@@ -247,6 +257,7 @@
 
 
 LINE = 4
+FAR_FIRST = 0x0312
 ORDER = (0, 4, 1, 3, 2, 5, 7, 6, 8, 9, 11, 10, 12, 13, 15, 14)
 
 

time: 24.5 us -> 24.2 us (0.988)
  Pallas kernels: 23.7 us -> 23.4 us
    pallas_call x1, Pallas kernels: 23.7 us -> 23.4 us  [shards(): pl.pallas_call(functools.partial(kernel, n_r, n_c), out_shape=jax.ShapeDt...]
where the time goes in v5:
time: 24.2 us; the launch traced here: 24.1 us
  Pallas kernels  23.4 us (97%)
  local copies, waits for them, and re-layouts  0.71 us (3%)
    pallas_call x1, Pallas kernels, shards(): pl.pallas_call(functools.partial(kernel, n_r, n_c), out_shape=jax.ShapeDt...  23.4 us
    unnamed x1, local copies, waits for them, and re-layouts  0.71 us

profile of v5, /device:TPU:0, one launch (start us, length us, event | category | flops | bytes accessed | tf_op | source)
XLA Modules:
  0.0 24.1 jit_solution(2516345850433768125)
XLA Ops:
  0.0 23.4 %shard_map.37 = f32[32,2048]{1,0:T(8,128)S(1)} custom-call(f32[32,256]{1,0:T(8,128)} %w_hbm.1, f32[2048,2048]{1,0:T(8,128)} %d_hbm.1, f32[32,2048]{1,0:T(8,128)} %h_hbm.1), custom_call_target="tpu_custom_call" | custom-call | flops 268435456 | bytes 16777216 | tf_op jit(solution)/shard_map/pallas_call | solution.py:272
  23.4 0.7 %copy.5 = f32[32,2048]{1,0:T(8,128)} copy(f32[32,2048]{1,0:T(8,128)S(1)} %shard_map.37) | data formatting | bytes 524288

commit v6 on v5

--- a/solution.py
+++ b/solution.py
@@ -216,6 +216,13 @@
                 spread[k, 8 * b : 8 * b + 8] = whole if b > b0 else jnp.where(subs > s0, whole, 0.0)
                 lower.add((k, b))
 
+    def o_copy(i, slot, first=0, n=rank):
+        cols = pl.ds(pl.multiple_of(slot * width, width), width)
+        return pltpu.make_async_remote_copy(
+            src_ref=hnew.at[first : first + n], dst_ref=out_ref.at[first : first + n, cols], send_sem=osend, recv_sem=orecv,
+            device_id=(i, c), device_id_type=MESH,
+        )
+
     all_partials = pltpu.make_async_copy(outbox.at[1:], inbox.at[1:], precv)
     all_partials.wait()
 
@@ -229,17 +236,21 @@
         for b in range(b0, blocks):
             if (k, b) in lower:
                 u[b] = u[b] - spread[k, 8 * b : 8 * b + 8] * fresh
+        if k == rank // 2 - 1:
+            hnew[: rank // 2] = jnp.maximum(jnp.concatenate(u[: blocks // 2], axis=0), 0.0)
+            for i in ORDER[:URGENT]:
+                @pl.when(i != r)
+                def _(i=i):
+                    o_copy(i, r, 0, rank // 2).start()
     fresh = jnp.maximum(jnp.concatenate(u, axis=0), 0.0)
-    hnew[...] = fresh
-
-    def o_copy(i, slot):
-        cols = pl.ds(pl.multiple_of(slot * width, width), width)
-        return pltpu.make_async_remote_copy(
-            src_ref=hnew, dst_ref=out_ref.at[:, cols], send_sem=osend, recv_sem=orecv,
-            device_id=(i, c), device_id_type=MESH,
-        )
-
-    for i in ORDER:
+    hnew[rank // 2 :] = fresh[rank // 2 :]
+
+    for i in ORDER[:URGENT]:
+        @pl.when(i != r)
+        def _():
+            o_copy(i, r, rank // 2, rank // 2).start()
+
+    for i in ORDER[URGENT:]:
         @pl.when(i != r)
         def _():
             o_copy(i, r).start()
@@ -257,6 +268,7 @@
 
 
 LINE = 4
+URGENT = 1
 FAR_FIRST = 0x0312
 ORDER = (0, 4, 1, 3, 2, 5, 7, 6, 8, 9, 11, 10, 12, 13, 15, 14)
 

time: 24.2 us -> 24.1 us (level)
  no operation moved by 1% of the time
where the time goes in v6:
time: 24.1 us; the launch traced here: 24 us
  Pallas kernels  23.3 us (97%)
  local copies, waits for them, and re-layouts  0.71 us (3%)
    pallas_call x1, Pallas kernels, shards(): pl.pallas_call(functools.partial(kernel, n_r, n_c), out_shape=jax.ShapeDt...  23.3 us
    unnamed x1, local copies, waits for them, and re-layouts  0.71 us

profile of v6, /device:TPU:0, one launch (start us, length us, event | category | flops | bytes accessed | tf_op | source)
XLA Modules:
  0.0 24.0 jit_solution(15196359024411205876)
XLA Ops:
  0.0 23.3 %shard_map.37 = f32[32,2048]{1,0:T(8,128)S(1)} custom-call(f32[32,256]{1,0:T(8,128)} %w_hbm.1, f32[2048,2048]{1,0:T(8,128)} %d_hbm.1, f32[32,2048]{1,0:T(8,128)} %h_hbm.1), custom_call_target="tpu_custom_call" | custom-call | flops 268435456 | bytes 16777216 | tf_op jit(solution)/shard_map/pallas_call | solution.py:284
  23.3 0.7 %copy.5 = f32[32,2048]{1,0:T(8,128)} copy(f32[32,2048]{1,0:T(8,128)S(1)} %shard_map.37) | data formatting | bytes 524288
